TPU v7x, 32 devices: a whole 2x2x4 slice. The times are simulated.
32 devices in a mesh: gx: 4 (over x, core), gy: 8 (over z, y).
Axes of the slice: x: 2, y: 2, z: 4, core: 2. Of those that a mesh axis runs over, the one named last changes fastest.
Arguments:
- nest_state: float32 [4, 8, 96, 3072], P(None, None, 'gx', 'gy'), may hold values from -6 to 6
- parent_state: float32 [4, 8, 96, 3072], P(None, None, 'gx', 'gy'), may hold values from -6 to 6
- offset_x: int32 [1], replicated, may hold values from 1 to 15
- offset_y: int32 [1], replicated, may hold values from 385 to 511
Outputs:
- nest_out: float32 [4, 8, 96, 3072], P(None, None, 'gx', 'gy')
- parent_out: float32 [4, 8, 96, 3072], P(None, None, 'gx', 'gy')
All inputs are finite; a program needn't handle non-finite values.
Results may differ from a plain program's by a relative error of at most 0.00019.
Values sent between devices are 32-bit elements; how exact they have to be, the bound alone decides.
A program may use at most 128 MiB of HBM per device.

v0:
```python
import jax
import jax.numpy as jnp
from jax import lax
from jax.sharding import PartitionSpec as P

SUBSTEPS = 3
CARRY_RATE = 0.35
SOUND_RATE = 0.4
MIXING_RATE = 0.2


def extended(value, sides, width):
    for axis, dim in sides:
        size, length = (lax.axis_size(axis), value.shape[dim])
        up = [(i, (i + 1) % size) for i in range(size - 1)]
        down = [(j, i) for i, j in up]
        last = lax.slice_in_dim(value, length - width, length, axis=dim)
        initial = lax.slice_in_dim(value, 0, width, axis=dim)
        before = lax.ppermute(last, axis, up)
        after = lax.ppermute(initial, axis, down)
        value = jnp.concatenate([before, value, after], axis=dim)
    return value


def advance(padded):
    center = padded[:, :, 1:-1, 1:-1]
    slope_x = (padded[:, :, 2:, 1:-1] - padded[:, :, :-2, 1:-1]) * 0.5
    slope_y = (padded[:, :, 1:-1, 2:] - padded[:, :, 1:-1, :-2]) * 0.5
    carried = center[0][None] * slope_x[:3] + center[1][None] * slope_y[:3]
    potential = center[2]
    level_above = jnp.concatenate([potential[1:], potential[-1:]], axis=0)
    level_below = jnp.concatenate([potential[:1], potential[:-1]], axis=0)
    wind_east = center[0] - CARRY_RATE * carried[0] - SOUND_RATE * slope_x[3]
    wind_north = center[1] - CARRY_RATE * carried[1] - SOUND_RATE * slope_y[3]
    heat_next = (
        potential
        - CARRY_RATE * carried[2]
        + MIXING_RATE * (level_above - 2.0 * potential + level_below)
    )
    pressure = center[3] - SOUND_RATE * (slope_x[0] + slope_y[1])
    return jnp.stack([wind_east, wind_north, heat_next, pressure])


def place_along(piece, first, width, axis):
    length = piece.shape[axis]
    target = lax.broadcasted_iota(jnp.int32, (length, width), 0) - first
    places = lax.broadcasted_iota(jnp.int32, (length, width), 1)
    table = (target == places).astype(jnp.float32)
    moved = jnp.moveaxis(piece, axis, -1)
    placed = jnp.dot(
        moved, table, precision=lax.Precision.HIGHEST, preferred_element_type=jnp.float32
    )
    return jnp.moveaxis(placed, -1, axis)


def on_device(nest_state, parent_state, offset_x, offset_y):
    shift_x = offset_x[0]
    shift_y = offset_y[0]
    count_x = lax.axis_size("gx")
    count_y = lax.axis_size("gy")
    index_x = lax.axis_index("gx")
    index_y = lax.axis_index("gy")
    levels = nest_state.shape[1]
    nest_cols = nest_state.shape[2]
    nest_rows = nest_state.shape[3]
    parent_cols = parent_state.shape[2]
    parent_rows = parent_state.shape[3]
    coarse_cols = nest_cols // 3
    coarse_rows = nest_rows // 3
    span_x = count_x * coarse_cols
    span_y = count_y * coarse_rows

    def take_slab(wanted, owner_index, extent, axis):
        local = wanted - owner_index * extent
        inside = (local >= 0) & (local < extent)
        slab = lax.dynamic_slice_in_dim(parent_state, jnp.clip(local, 0, extent - 1), 1, axis)
        return jnp.where(inside, jnp.squeeze(slab, axis), 0.0)

    columns = jnp.stack(
        [
            take_slab(shift_x - 1, index_x, parent_cols, 2),
            take_slab(shift_x + span_x, index_x, parent_cols, 2),
        ]
    )
    columns = lax.psum(columns, "gx")
    row_pair = jnp.stack(
        [
            take_slab(shift_y - 1, index_y, parent_rows, 3),
            take_slab(shift_y + span_y, index_y, parent_rows, 3),
        ]
    )
    row_pair = lax.psum(row_pair, "gy")
    column_first = shift_y + index_y * coarse_rows - 1
    row_first = shift_x + index_x * coarse_cols - 1
    column_strip = place_along(
        lax.all_gather(columns, "gy", axis=3, tiled=True), column_first, coarse_rows + 2, 3
    )
    row_strip = place_along(
        lax.all_gather(row_pair, "gx", axis=3, tiled=True), row_first, coarse_cols + 2, 3
    )
    column_strip = jnp.repeat(column_strip, 3, axis=3)
    row_strip = jnp.repeat(row_strip, 3, axis=3)
    parent_padded = extended(parent_state, (("gx", 2), ("gy", 3)), 1)
    parent_next = advance(parent_padded)
    fields = nest_state
    for substep in range(SUBSTEPS):
        padded = extended(fields, (("gx", 2), ("gy", 3)), 1)
        col_pos = lax.broadcasted_iota(jnp.int32, (padded.shape[2], 1), 0)
        row_pos = lax.broadcasted_iota(jnp.int32, (1, padded.shape[3]), 1)
        lower = 3 - 1
        west = column_strip[0][:, :, None, lower : lower + nest_rows + 2 * 1]
        east = column_strip[1][:, :, None, lower : lower + nest_rows + 2 * 1]
        south = row_strip[0][:, :, lower : lower + nest_cols + 2 * 1, None]
        north = row_strip[1][:, :, lower : lower + nest_cols + 2 * 1, None]
        result = jnp.where((index_x == 0) & (col_pos < 1), west, padded)
        result = jnp.where((index_x == count_x - 1) & (col_pos >= nest_cols + 1), east, result)
        result = jnp.where((index_y == 0) & (row_pos < 1), south, result)
        result = jnp.where((index_y == count_y - 1) & (row_pos >= nest_rows + 1), north, result)
        fields = advance(result)
    coarse = fields[:3].reshape(3, levels, coarse_cols, 3, coarse_rows, 3).mean(axis=(3, 5))
    col_first = index_x * parent_cols - shift_x
    rows_first = index_y * parent_rows - shift_y
    partial_block = place_along(
        lax.all_gather(coarse, "gy", axis=3, tiled=True), rows_first, parent_rows, 3
    )
    returned = place_along(
        lax.all_gather(partial_block, "gx", axis=2, tiled=True), col_first, parent_cols, 2
    )
    col_global = index_x * parent_cols + lax.broadcasted_iota(jnp.int32, (parent_cols, 1), 0)
    row_global = index_y * parent_rows + lax.broadcasted_iota(jnp.int32, (1, parent_rows), 1)
    inside = (
        (col_global >= shift_x)
        & (col_global < shift_x + span_x)
        & (row_global >= shift_y)
        & (row_global < shift_y + span_y)
    )
    blended = jnp.where(inside, returned, parent_next[:3])
    parent_out = jnp.concatenate([blended, parent_next[3:]], axis=0)
    return (fields, parent_out)


def solution(mesh):
    placed = (P(None, None, "gx", "gy"), P(None, None, "gx", "gy"), P(), P())
    return jax.shard_map(
        on_device,
        mesh=mesh,
        in_specs=placed,
        out_specs=(P(None, None, "gx", "gy"), P(None, None, "gx", "gy")),
        check_vma=False,
    )
```

profile of v0, /device:TPU:0, one launch (start us, length us, event | category | flops | bytes accessed | tf_op | source)
XLA Modules:
  0.0 323.4 jit_solution(11506212641012016978)
XLA Ops:
  8.0 2.2 fusion.95
  10.2 0.7 pad_maximum_fusion.29
  10.9 1.2 fusion.96
  12.1 2.4 collective-permute-start
  14.4 1.3 collective-permute-start.1
  17.4 39.1 %psum.14 = f32[2,4,8,24]{2,1,0,3:T(4,128)S(1)} all-reduce(f32[2,4,8,24]{2,1,0,3:T(4,128)S(1)} %copy.41), channel_id=1, replica_groups=mesh['gx'=4,'gy'=8] {'gy'}, use_global_device_ids=true, to_apply=%region_0.1 | all-reduce | flops 1536 | bytes 12288 | tf_op jit(solution)/shard_map/psum | solution.py:92
  56.5 9.2 %all_gather.12 = f32[2,4,8,96]{2,1,0,3:T(4,128)S(1)} all-gather(f32[2,4,8,24]{2,1,0,3:T(4,128)S(1)} %psum.14), channel_id=1, replica_groups=mesh['gx'=4,'gy'=8] {'gx'}, dimensions={3}, use_global_device_ids=true | all-gather | bytes 30720 | tf_op jit(solution)/shard_map/all_gather | solution.py:99
  66.6 1.3 pad_maximum_fusion.28
  67.9 2.1 collective-permute-start.2
  70.0 1.3 collective-permute-start.3
  71.3 50.3 %all_gather.13 = f32[2,4,8,3072]{3,2,1,0:T(8,128)S(1)} all-gather(f32[2,4,8,384]{3,2,1,0:T(8,128)} %all-reduce.2.cloned.1.call-done), channel_id=1, replica_groups=mesh['gx'=4,'gy'=8] {'gy'}, dimensions={3}, use_global_device_ids=true | all-gather | bytes 884736 | tf_op jit(solution)/shard_map/all_gather | solution.py:96
  121.6 1.1 fusion.10
  124.2 3.1 fusion.2
  127.2 1.0 fusion.25
  129.6 1.3 collective-permute-start.4
  130.9 1.3 collective-permute-start.5
  132.2 1.3 collective-permute-start.12
  133.5 5.1 %collective-permute-start.13 = (f32[4,8,1,384]{3,2,1,0:T(1,128)}, f32[4,8,1,384]{3,2,1,0:T(1,128)S(1)}, u32[]{:S(2)}, u32[]{:S(2)}) collective-permute-start(f32[4,8,1,384]{3,2,1,0:T(1,128)} %get-tuple-element.58), channel_id=1, source_target_pairs={{0,8},{8,16},{16,24},{1,9},{9,17},{17,25},{2,10},{10,18},{18,26},{... | collective-permute-start | bytes 147464 | tf_op jit(solution)/shard_map/ppermute | solution.py:19
  138.9 1.3 collective-permute-start.6
  140.3 1.5 collective-permute-start.7
  141.8 0.8 fusion.94
  142.6 20.1 %collective-permute-done.6 = f32[4,8,26,1]{3,2,1,0:T(8,128)S(1)} collective-permute-done((f32[4,8,26,1]{3,2,1,0:T(8,128)S(1)}, f32[4,8,26,1]{3,2,1,0:T(8,128)S(1)}, u32[]{:S(2)}, u32[]{:S(2)}) %collective-permute-start.6) | collective-permute-done | bytes 3360 | tf_op jit(solution)/shard_map/ppermute | solution.py:19
  162.7 2.6 fusion.5
  165.4 1.0 fusion.23
  167.7 3.1 collective-permute-start.8
  170.8 1.3 collective-permute-start.9
  172.7 1.5 collective-permute-done.9
  174.5 4.4 %collective-permute-start.10 = (f32[4,8,26,1]{3,2,1,0:T(8,128)S(1)}, f32[4,8,26,1]{3,2,1,0:T(8,128)S(1)}, u32[]{:S(2)}, u32[]{:S(2)}) collective-permute-start(f32[4,8,26,1]{3,2,1,0:T(8,128)S(1)} %get-tuple-element.46), channel_id=1, source_target_pairs={{0,1},{1,2},{2,3},{3,4},{4,5},{5,6},{6,7},{8,9},{9,10},{10,11},{11... | collective-permute-start | bytes 9992 | tf_op jit(solution)/shard_map/ppermute | solution.py:19
  178.9 1.3 collective-permute-start.11
  180.3 20.3 %collective-permute-done.10 = f32[4,8,26,1]{3,2,1,0:T(8,128)S(1)} collective-permute-done((f32[4,8,26,1]{3,2,1,0:T(8,128)S(1)}, f32[4,8,26,1]{3,2,1,0:T(8,128)S(1)}, u32[]{:S(2)}, u32[]{:S(2)}) %collective-permute-start.10) | collective-permute-done | bytes 3360 | tf_op jit(solution)/shard_map/ppermute | solution.py:19
  200.6 2.6 fusion.8
  203.2 1.0 fusion.21
  204.9 1.2 fusion.49
  206.2 8.3 %copy.53 = f32[3,8,24,384]{1,3,2,0:T(8,128)} copy(f32[3,8,24,384]{3,2,1,0:T(8,128)S(1)} %pad_maximum_fusion.10) | data formatting | bytes 1769472 | tf_op jit(solution)/shard_map/stack | solution.py:41
  214.4 21.9 %reshape.170 = f32[3,8,8,3,128,3]{1,5,4,3,2,0:T(4,128)} reshape(f32[3,8,24,384]{1,3,2,0:T(8,128)} %copy.53) | data formatting | bytes 1769472 | tf_op jit(solution)/shard_map/reshape | solution.py:120
  236.3 14.8 %reduce_sum.9 = f32[3,8,8,128]{1,3,2,0:T(8,128)S(1)} reduce(f32[3,8,8,3,128,3]{1,5,4,3,2,0:T(4,128)} %reshape.170, f32[]{:T(128)} %constant.17.clone.1), dimensions={3,5}, to_apply=%region_2.3 | reduce | flops 196608 | bytes 983044 | tf_op jit(solution)/shard_map/reduce_sum | solution.py:120
  251.6 36.0 %all_gather.14 = f32[3,8,8,1024]{3,2,1,0:T(8,128)S(1)} all-gather(f32[3,8,8,128]{3,2,1,0:T(8,128)S(1)} %broadcast_multiply_fusion), channel_id=1, replica_groups=mesh['gx'=4,'gy'=8] {'gy'}, dimensions={3}, use_global_device_ids=true | all-gather | bytes 884736 | tf_op jit(solution)/shard_map/all_gather | solution.py:124
  287.6 1.7 fusion.13
  289.8 1.3 collective-permute-start.14
  291.1 4.6 %collective-permute-start.15 = (f32[4,8,26,1]{3,2,1,0:T(8,128)S(1)}, f32[4,8,26,1]{3,2,1,0:T(8,128)S(1)}, u32[]{:S(2)}, u32[]{:S(2)}) collective-permute-start(f32[4,8,26,1]{3,2,1,0:T(8,128)S(1)} %get-tuple-element.45), channel_id=1, source_target_pairs={{0,1},{1,2},{2,3},{3,4},{4,5},{5,6},{6,7},{8,9},{9,10},{10,11},{11... | collective-permute-start | bytes 9992 | tf_op jit(solution)/shard_map/ppermute | solution.py:19
  295.7 5.2 %collective-permute-done.14 = f32[4,8,26,1]{3,2,1,0:T(8,128)S(1)} collective-permute-done((f32[4,8,26,1]{3,2,1,0:T(8,128)S(1)}, f32[4,8,26,1]{3,2,1,0:T(8,128)S(1)}, u32[]{:S(2)}, u32[]{:S(2)}) %collective-permute-start.14) | collective-permute-done | bytes 3360 | tf_op jit(solution)/shard_map/ppermute | solution.py:20
  300.9 8.2 %collective-permute-done.15 = f32[4,8,26,1]{3,2,1,0:T(8,128)S(1)} collective-permute-done((f32[4,8,26,1]{3,2,1,0:T(8,128)S(1)}, f32[4,8,26,1]{3,2,1,0:T(8,128)S(1)}, u32[]{:S(2)}, u32[]{:S(2)}) %collective-permute-start.15) | collective-permute-done | bytes 3360 | tf_op jit(solution)/shard_map/ppermute | solution.py:19
  309.2 1.2 fusion.19
  310.6 0.8 copy-done.6
  311.5 1.0 fusion.41
  312.5 1.1 pad_maximum_fusion.8
  313.6 1.8 fusion.15
  315.5 1.1 pad_maximum_fusion.9
  (96 shorter events, 9.1 us)
Async XLA Ops:
  7.2 9.3 %copy-start = (f32[4,8,24,384]{3,2,1,0:T(8,128)S(1)}, f32[4,8,24,384]{3,2,1,0:T(8,128)}, u32[]{:S(2)}) copy-start(f32[4,8,24,384]{3,2,1,0:T(8,128)} %param.5) | copy-start | bytes 3538948
  7.2 64.1 %all-reduce.2.cloned.1.call-start = ((), (), s32[]{:S(2)}) async-start(), calls=%async_computation | async-start | bytes 196608 | tf_op jit(solution)/shard_map/psum | solution.py:85
  10.8 302.8 %all-gather.2.cloned.1.call-start = ((), (), s32[]{:S(2)}) async-start(), calls=%async_computation.1 | async-start | bytes 1474560 | tf_op jit(solution)/shard_map/all_gather | solution.py:127
  12.1 54.6 %collective-permute-start = (f32[4,8,1,384]{3,2,1,0:T(1,128)S(1)}, f32[4,8,1,384]{3,2,1,0:T(1,128)S(1)}, u32[]{:S(2)}, u32[]{:S(2)}) collective-permute-start(f32[4,8,1,384]{3,2,1,0:T(1,128)S(1)} %get-tuple-element.68), channel_id=1, source_target_pairs={{0,8},{8,16},{16,24},{1,9},{9,17},{17,25},{2,10},{10,18},{18,26},{... | collective-permute-start | bytes 147464 | tf_op jit(solution)/shard_map/ppermute | solution.py:19
  14.4 52.2 %collective-permute-start.1 = (f32[4,8,1,384]{3,2,1,0:T(1,128)S(1)}, f32[4,8,1,384]{3,2,1,0:T(1,128)S(1)}, u32[]{:S(2)}, u32[]{:S(2)}) collective-permute-start(f32[4,8,1,384]{3,2,1,0:T(1,128)S(1)} %get-tuple-element.69), channel_id=1, source_target_pairs={{8,0},{16,8},{24,16},{9,1},{17,9},{25,17},{10,2},{18,10},{26,18},{... | collective-permute-start | bytes 147464 | tf_op jit(solution)/shard_map/ppermute | solution.py:20
  17.0 49.7 %copy-start.1 = (f32[4,8,24,384]{3,2,1,0:T(8,128)S(1)}, f32[4,8,24,384]{3,2,1,0:T(8,128)}, u32[]{:S(2)}) copy-start(f32[4,8,24,384]{3,2,1,0:T(8,128)} %param.4) | copy-start | bytes 3538948
  67.9 56.3 %collective-permute-start.2 = (f32[4,8,26,1]{3,2,1,0:T(8,128)}, f32[4,8,26,1]{3,2,1,0:T(8,128)}, u32[]{:S(2)}, u32[]{:S(2)}) collective-permute-start(f32[4,8,26,1]{3,2,1,0:T(8,128)} %get-tuple-element.50), channel_id=1, source_target_pairs={{0,1},{1,2},{2,3},{3,4},{4,5},{5,6},{6,7},{8,9},{9,10},{10,11},{11... | collective-permute-start | bytes 9992 | tf_op jit(solution)/shard_map/ppermute | solution.py:19
  70.0 54.2 %collective-permute-start.3 = (f32[4,8,26,1]{3,2,1,0:T(8,128)}, f32[4,8,26,1]{3,2,1,0:T(8,128)}, u32[]{:S(2)}, u32[]{:S(2)}) collective-permute-start(f32[4,8,26,1]{3,2,1,0:T(8,128)} %get-tuple-element.51), channel_id=1, source_target_pairs={{1,0},{2,1},{3,2},{4,3},{5,4},{6,5},{7,6},{9,8},{10,9},{11,10},{12... | collective-permute-start | bytes 9992 | tf_op jit(solution)/shard_map/ppermute | solution.py:20
  129.6 9.0 %collective-permute-start.4 = (f32[4,8,1,384]{3,2,1,0:T(1,128)S(1)}, f32[4,8,1,384]{3,2,1,0:T(1,128)S(1)}, u32[]{:S(2)}, u32[]{:S(2)}) collective-permute-start(f32[4,8,1,384]{3,2,1,0:T(1,128)S(1)} %get-tuple-element.64), channel_id=1, source_target_pairs={{0,8},{8,16},{16,24},{1,9},{9,17},{17,25},{2,10},{10,18},{18,26},{... | collective-permute-start | bytes 147464 | tf_op jit(solution)/shard_map/ppermute | solution.py:19
  130.9 7.7 %collective-permute-start.5 = (f32[4,8,1,384]{3,2,1,0:T(1,128)S(1)}, f32[4,8,1,384]{3,2,1,0:T(1,128)S(1)}, u32[]{:S(2)}, u32[]{:S(2)}) collective-permute-start(f32[4,8,1,384]{3,2,1,0:T(1,128)S(1)} %get-tuple-element.65), channel_id=1, source_target_pairs={{8,0},{16,8},{24,16},{9,1},{17,9},{25,17},{10,2},{18,10},{26,18},{... | collective-permute-start | bytes 147464 | tf_op jit(solution)/shard_map/ppermute | solution.py:20
  132.2 157.3 %collective-permute-start.12 = (f32[4,8,1,384]{3,2,1,0:T(1,128)}, f32[4,8,1,384]{3,2,1,0:T(1,128)S(1)}, u32[]{:S(2)}, u32[]{:S(2)}) collective-permute-start(f32[4,8,1,384]{3,2,1,0:T(1,128)} %get-tuple-element.59), channel_id=1, source_target_pairs={{8,0},{16,8},{24,16},{9,1},{17,9},{25,17},{10,2},{18,10},{26,18},{... | collective-permute-start | bytes 147464 | tf_op jit(solution)/shard_map/ppermute | solution.py:20
  133.5 156.0 %collective-permute-start.13 = (f32[4,8,1,384]{3,2,1,0:T(1,128)}, f32[4,8,1,384]{3,2,1,0:T(1,128)S(1)}, u32[]{:S(2)}, u32[]{:S(2)}) collective-permute-start(f32[4,8,1,384]{3,2,1,0:T(1,128)} %get-tuple-element.58), channel_id=1, source_target_pairs={{0,8},{8,16},{16,24},{1,9},{9,17},{17,25},{2,10},{10,18},{18,26},{... | collective-permute-start | bytes 147464 | tf_op jit(solution)/shard_map/ppermute | solution.py:19
  138.9 23.8 %collective-permute-start.6 = (f32[4,8,26,1]{3,2,1,0:T(8,128)S(1)}, f32[4,8,26,1]{3,2,1,0:T(8,128)S(1)}, u32[]{:S(2)}, u32[]{:S(2)}) collective-permute-start(f32[4,8,26,1]{3,2,1,0:T(8,128)S(1)} %get-tuple-element.48), channel_id=1, source_target_pairs={{0,1},{1,2},{2,3},{3,4},{4,5},{5,6},{6,7},{8,9},{9,10},{10,11},{11... | collective-permute-start | bytes 9992 | tf_op jit(solution)/shard_map/ppermute | solution.py:19
  140.3 22.5 %collective-permute-start.7 = (f32[4,8,26,1]{3,2,1,0:T(8,128)S(1)}, f32[4,8,26,1]{3,2,1,0:T(8,128)S(1)}, u32[]{:S(2)}, u32[]{:S(2)}) collective-permute-start(f32[4,8,26,1]{3,2,1,0:T(8,128)S(1)} %get-tuple-element.49), channel_id=1, source_target_pairs={{1,0},{2,1},{3,2},{4,3},{5,4},{6,5},{7,6},{9,8},{10,9},{11,10},{12... | collective-permute-start | bytes 9992 | tf_op jit(solution)/shard_map/ppermute | solution.py:20
  167.7 5.0 %collective-permute-start.8 = (f32[4,8,1,384]{3,2,1,0:T(1,128)S(1)}, f32[4,8,1,384]{3,2,1,0:T(1,128)S(1)}, u32[]{:S(2)}, u32[]{:S(2)}) collective-permute-start(f32[4,8,1,384]{3,2,1,0:T(1,128)S(1)} %get-tuple-element.62), channel_id=1, source_target_pairs={{0,8},{8,16},{16,24},{1,9},{9,17},{17,25},{2,10},{10,18},{18,26},{... | collective-permute-start | bytes 147464 | tf_op jit(solution)/shard_map/ppermute | solution.py:19
  170.8 3.4 %collective-permute-start.9 = (f32[4,8,1,384]{3,2,1,0:T(1,128)S(1)}, f32[4,8,1,384]{3,2,1,0:T(1,128)S(1)}, u32[]{:S(2)}, u32[]{:S(2)}) collective-permute-start(f32[4,8,1,384]{3,2,1,0:T(1,128)S(1)} %get-tuple-element.63), channel_id=1, source_target_pairs={{8,0},{16,8},{24,16},{9,1},{17,9},{25,17},{10,2},{18,10},{26,18},{... | collective-permute-start | bytes 147464 | tf_op jit(solution)/shard_map/ppermute | solution.py:20
  174.5 26.0 %collective-permute-start.10 = (f32[4,8,26,1]{3,2,1,0:T(8,128)S(1)}, f32[4,8,26,1]{3,2,1,0:T(8,128)S(1)}, u32[]{:S(2)}, u32[]{:S(2)}) collective-permute-start(f32[4,8,26,1]{3,2,1,0:T(8,128)S(1)} %get-tuple-element.46), channel_id=1, source_target_pairs={{0,1},{1,2},{2,3},{3,4},{4,5},{5,6},{6,7},{8,9},{9,10},{10,11},{11... | collective-permute-start | bytes 9992 | tf_op jit(solution)/shard_map/ppermute | solution.py:19
  178.9 21.6 %collective-permute-start.11 = (f32[4,8,26,1]{3,2,1,0:T(8,128)S(1)}, f32[4,8,26,1]{3,2,1,0:T(8,128)S(1)}, u32[]{:S(2)}, u32[]{:S(2)}) collective-permute-start(f32[4,8,26,1]{3,2,1,0:T(8,128)S(1)} %get-tuple-element.47), channel_id=1, source_target_pairs={{1,0},{2,1},{3,2},{4,3},{5,4},{6,5},{7,6},{9,8},{10,9},{11,10},{12... | collective-permute-start | bytes 9992 | tf_op jit(solution)/shard_map/ppermute | solution.py:20
  206.1 8.3 %copy-start.2 = (f32[1,8,24,384]{3,2,1,0:T(8,128)}, f32[1,8,24,384]{3,2,1,0:T(8,128)S(1)}, u32[]{:S(2)}) copy-start(f32[1,8,24,384]{3,2,1,0:T(8,128)S(1)} %get-tuple-element.11) | copy-start | bytes 884740
  289.8 11.1 %collective-permute-start.14 = (f32[4,8,26,1]{3,2,1,0:T(8,128)S(1)}, f32[4,8,26,1]{3,2,1,0:T(8,128)S(1)}, u32[]{:S(2)}, u32[]{:S(2)}) collective-permute-start(f32[4,8,26,1]{3,2,1,0:T(8,128)S(1)} %get-tuple-element.44), channel_id=1, source_target_pairs={{1,0},{2,1},{3,2},{4,3},{5,4},{6,5},{7,6},{9,8},{10,9},{11,10},{12... | collective-permute-start | bytes 9992 | tf_op jit(solution)/shard_map/ppermute | solution.py:20
  291.1 18.0 %collective-permute-start.15 = (f32[4,8,26,1]{3,2,1,0:T(8,128)S(1)}, f32[4,8,26,1]{3,2,1,0:T(8,128)S(1)}, u32[]{:S(2)}, u32[]{:S(2)}) collective-permute-start(f32[4,8,26,1]{3,2,1,0:T(8,128)S(1)} %get-tuple-element.45), channel_id=1, source_target_pairs={{0,1},{1,2},{2,3},{3,4},{4,5},{5,6},{6,7},{8,9},{9,10},{10,11},{11... | collective-permute-start | bytes 9992 | tf_op jit(solution)/shard_map/ppermute | solution.py:19
  310.4 0.9 copy-start.6
  310.4 1.1 copy-start.7
  310.4 1.1 copy-start.8
  310.4 1.1 copy-start.9
  311.5 1.0 copy-start.3
  311.5 1.0 copy-start.4
  312.5 1.1 copy-start.5
Sparse Core Ops, SparseCore 0:
  11.0 34.0 all-reduce.1
  289.5 15.4 all-gather.1
where the time goes:
time: 325 us; the launch traced here: 323 us
  blocking collectives  135 us (42%)
  waiting for transfers between devices  55.4 us (17%)
  local copies, waits for them, and re-layouts  40.7 us (13%)
  other arithmetic  36.6 us (11%)
  starting transfers between devices  34.8 us (11%)
  between operations  16.1 us (5%)
  matrix products  5.11 us (2%)
    all_gather x1, blocking collectives, on_device(): lax.all_gather(columns, 'gy', axis=3, tiled=True)  50.3 us
    ppermute x8, waiting for transfers between devices, extended(): before = lax.ppermute(last, axis, up)  48.7 us
    psum x1, blocking collectives, on_device(): row_pair = lax.psum(row_pair, 'gy')  39.1 us
    all_gather x1, blocking collectives, on_device(): lax.all_gather(coarse, 'gy', axis=3, tiled=True)  36 us
    ppermute x8, starting transfers between devices, extended(): before = lax.ppermute(last, axis, up)  24.2 us
    reshape x1, local copies, waits for them, and re-layouts, on_device(): fields[:3].reshape(3, levels, coarse_cols, 3, coarse_rows, 3)  21.9 us
    reduce_sum x1, other arithmetic, on_device(): fields[:3].reshape(3, levels, coarse_cols, 3, coarse_rows, 3)  14.8 us
    ppermute x8, starting transfers between devices, extended(): after = lax.ppermute(initial, axis, down)  10.5 us
  transfers between devices with their start and end apart: 18, of which 5 were waited for; matrix products, arithmetic and copies ran while one was open for 22% of the time, Pallas kernels for 0%

commit v1 on v0

--- a/solution.py
+++ b/solution.py
@@ -7,6 +7,28 @@
 CARRY_RATE = 0.35
 SOUND_RATE = 0.4
 MIXING_RATE = 0.2
+
+
+def laid_out(blocks, dim):
+    shape = list(blocks.shape[1:])
+    shape[dim] *= blocks.shape[0]
+    return jnp.moveaxis(blocks, 0, dim).reshape(shape)
+
+
+def doubled(x, axis):
+    size = lax.axis_size(axis)
+    blocks = x[None]
+    for level in range(size.bit_length() - 1):
+        bit = 1 << level
+        other = lax.ppermute(blocks, axis, [(i, i ^ bit) for i in range(size)])
+        both = jnp.stack([blocks, other])
+        upper = lax.axis_index(axis) >> level & 1
+        blocks = jnp.where(upper == 0, both, both[::-1]).reshape(-1, *x.shape)
+    return blocks
+
+
+def gather_by_bits(x, axis, dim):
+    return laid_out(doubled(x, axis), dim)
 
 
 def extended(value, sides, width):
@@ -120,9 +142,7 @@
     coarse = fields[:3].reshape(3, levels, coarse_cols, 3, coarse_rows, 3).mean(axis=(3, 5))
     col_first = index_x * parent_cols - shift_x
     rows_first = index_y * parent_rows - shift_y
-    partial_block = place_along(
-        lax.all_gather(coarse, "gy", axis=3, tiled=True), rows_first, parent_rows, 3
-    )
+    partial_block = place_along(gather_by_bits(coarse, "gy", 3), rows_first, parent_rows, 3)
     returned = place_along(
         lax.all_gather(partial_block, "gx", axis=2, tiled=True), col_first, parent_cols, 2
     )

time: 325 us -> 342 us (1.052)
  blocking collectives: 135 us -> 98.6 us
  waiting for transfers between devices: 55.4 us -> 86 us
  starting transfers between devices: 34.8 us -> 43.2 us
  local copies, waits for them, and re-layouts: 40.7 us -> 48 us
  other arithmetic: 36.6 us -> 43.3 us
    all_gather x1 -> x0, blocking collectives: 36 us -> none  [on_device(): lax.all_gather(coarse, 'gy', axis=3, tiled=True)]
    ppermute x0 -> x3, waiting for transfers between devices: none -> 20.2 us  [doubled(): other = lax.ppermute(blocks, axis, [(i, i ^ bit) for i in range(size)])]
    ppermute x0 -> x3, starting transfers between devices: none -> 9.62 us  [doubled(): other = lax.ppermute(blocks, axis, [(i, i ^ bit) for i in range(size)])]
    ppermute x8, waiting for transfers between devices: 6.69 us -> 14.9 us  [extended(): after = lax.ppermute(initial, axis, down)]
    another operation x0 -> x4, other arithmetic: none -> 5.33 us  [doubled(): both = jnp.stack([blocks, other])]
  transfers between devices with their start and end apart: 18 -> 21, of which waited for: 5 -> 8; matrix products, arithmetic and copies ran while one was open for 22% -> 5% of each run, Pallas kernels for 0% -> 0%
where the time goes in v1:
time: 342 us; the launch traced here: 340 us
  blocking collectives  98.6 us (29%)
  waiting for transfers between devices  86 us (25%)
  local copies, waits for them, and re-layouts  48 us (14%)
  other arithmetic  43.3 us (13%)
  starting transfers between devices  43.2 us (13%)
  between operations  16.1 us (5%)
  matrix products  5.09 us (1%)
    ppermute x8, waiting for transfers between devices, extended(): before = lax.ppermute(last, axis, up)  50.8 us
    all_gather x1, blocking collectives, on_device(): lax.all_gather(columns, 'gy', axis=3, tiled=True)  50.3 us
    psum x1, blocking collectives, on_device(): row_pair = lax.psum(row_pair, 'gy')  39.1 us
    ppermute x8, starting transfers between devices, extended(): before = lax.ppermute(last, axis, up)  23 us
    reshape x1, local copies, waits for them, and re-layouts, on_device(): fields[:3].reshape(3, levels, coarse_cols, 3, coarse_rows, 3)  21.9 us
    ppermute x3, waiting for transfers between devices, doubled(): other = lax.ppermute(blocks, axis, [(i, i ^ bit) for i in range(size)])  20.2 us
    ppermute x8, waiting for transfers between devices, extended(): after = lax.ppermute(initial, axis, down)  14.9 us
    reduce_sum x1, other arithmetic, on_device(): fields[:3].reshape(3, levels, coarse_cols, 3, coarse_rows, 3)  14.8 us
  transfers between devices with their start and end apart: 21, of which 8 were waited for; matrix products, arithmetic and copies ran while one was open for 5% of the time, Pallas kernels for 0%

profile of v1, /device:TPU:0, one launch (start us, length us, event | category | flops | bytes accessed | tf_op | source)
XLA Modules:
  0.0 340.3 jit_solution(8165883914323433441)
XLA Ops:
  8.0 2.2 fusion.97
  12.0 2.4 collective-permute-start
  14.4 1.3 collective-permute-start.1
  17.4 39.1 %psum.14 = f32[2,4,8,24]{2,1,0,3:T(4,128)S(1)} all-reduce(f32[2,4,8,24]{2,1,0,3:T(4,128)S(1)} %copy.64), channel_id=1, replica_groups=mesh['gx'=4,'gy'=8] {'gy'}, use_global_device_ids=true, to_apply=%region_0.1 | all-reduce | flops 1536 | bytes 12288 | tf_op jit(solution)/shard_map/psum | solution.py:114
  56.5 9.2 %all_gather.9 = f32[2,4,8,96]{2,1,0,3:T(4,128)S(1)} all-gather(f32[2,4,8,24]{2,1,0,3:T(4,128)S(1)} %psum.14), channel_id=1, replica_groups=mesh['gx'=4,'gy'=8] {'gx'}, dimensions={3}, use_global_device_ids=true | all-gather | bytes 30720 | tf_op jit(solution)/shard_map/all_gather | solution.py:121
  66.6 1.3 pad_maximum_fusion.30
  67.9 2.1 collective-permute-start.2
  70.0 1.3 collective-permute-start.3
  71.3 50.3 %all_gather.10 = f32[2,4,8,3072]{3,2,1,0:T(8,128)S(1)} all-gather(f32[2,4,8,384]{3,2,1,0:T(8,128)} %all-reduce.2.cloned.1.call-done), channel_id=1, replica_groups=mesh['gx'=4,'gy'=8] {'gy'}, dimensions={3}, use_global_device_ids=true | all-gather | bytes 884736 | tf_op jit(solution)/shard_map/all_gather | solution.py:118
  124.1 3.1 fusion.4
  129.6 1.3 collective-permute-start.4
  130.9 1.3 collective-permute-start.5
  132.2 3.2 collective-permute-done.5
  135.8 1.3 collective-permute-start.6
  137.1 1.5 collective-permute-start.7
  138.6 19.9 %collective-permute-done.6 = f32[4,8,26,1]{3,2,1,0:T(8,128)S(1)} collective-permute-done((f32[4,8,26,1]{3,2,1,0:T(8,128)S(1)}, f32[4,8,26,1]{3,2,1,0:T(8,128)S(1)}, u32[]{:S(2)}, u32[]{:S(2)}) %collective-permute-start.6) | collective-permute-done | bytes 3360 | tf_op jit(solution)/shard_map/ppermute | solution.py:41
  158.4 2.6 fusion.7
  163.5 4.2 %collective-permute-start.8 = (f32[4,8,1,384]{3,2,1,0:T(1,128)S(1)}, f32[4,8,1,384]{3,2,1,0:T(1,128)S(1)}, u32[]{:S(2)}, u32[]{:S(2)}) collective-permute-start(f32[4,8,1,384]{3,2,1,0:T(1,128)S(1)} %get-tuple-element.66), channel_id=1, source_target_pairs={{0,8},{8,16},{16,24},{1,9},{9,17},{17,25},{2,10},{10,18},{18,26},{... | collective-permute-start | bytes 147464 | tf_op jit(solution)/shard_map/ppermute | solution.py:41
  167.7 1.3 collective-permute-start.9
  169.0 1.8 collective-permute-done.9
  171.1 4.1 %collective-permute-start.10 = (f32[4,8,26,1]{3,2,1,0:T(8,128)S(1)}, f32[4,8,26,1]{3,2,1,0:T(8,128)S(1)}, u32[]{:S(2)}, u32[]{:S(2)}) collective-permute-start(f32[4,8,26,1]{3,2,1,0:T(8,128)S(1)} %get-tuple-element.50), channel_id=1, source_target_pairs={{0,1},{1,2},{2,3},{3,4},{4,5},{5,6},{6,7},{8,9},{9,10},{10,11},{11... | collective-permute-start | bytes 9992 | tf_op jit(solution)/shard_map/ppermute | solution.py:41
  175.2 1.3 collective-permute-start.11
  176.5 20.7 %collective-permute-done.10 = f32[4,8,26,1]{3,2,1,0:T(8,128)S(1)} collective-permute-done((f32[4,8,26,1]{3,2,1,0:T(8,128)S(1)}, f32[4,8,26,1]{3,2,1,0:T(8,128)S(1)}, u32[]{:S(2)}, u32[]{:S(2)}) %collective-permute-start.10) | collective-permute-done | bytes 3360 | tf_op jit(solution)/shard_map/ppermute | solution.py:41
  197.2 2.6 fusion.10
  201.5 1.2 fusion.51
  202.8 8.3 %copy.76 = f32[3,8,24,384]{1,3,2,0:T(8,128)} copy(f32[3,8,24,384]{3,2,1,0:T(8,128)S(1)} %pad_maximum_fusion.11) | data formatting | bytes 1769472 | tf_op jit(solution)/shard_map/stack | solution.py:63
  211.1 21.9 %reshape.200 = f32[3,8,8,3,128,3]{1,5,4,3,2,0:T(4,128)} reshape(f32[3,8,24,384]{1,3,2,0:T(8,128)} %copy.76) | data formatting | bytes 1769472 | tf_op jit(solution)/shard_map/reshape | solution.py:142
  232.9 14.8 %reduce_sum.9 = f32[3,8,8,128]{1,3,2,0:T(8,128)S(1)} reduce(f32[3,8,8,3,128,3]{1,5,4,3,2,0:T(4,128)} %reshape.200, f32[]{:T(128)} %constant.17.clone.1), dimensions={3,5}, to_apply=%region_2.3 | reduce | flops 196608 | bytes 983044 | tf_op jit(solution)/shard_map/reduce_sum | solution.py:142
  247.7 2.0 multiply_bitcast_fusion.1
  249.7 1.8 copy.77
  251.6 2.5 collective-permute-start.12
  254.1 3.0 collective-permute-done.12
  257.6 1.7 pad_maximum_fusion
  259.3 3.5 %fusion.1 = (f32[1,2,3,8,8,128]{3,5,4,2,1,0:T(8,128)}, f32[2,3,8,8,128]{2,4,3,1,0:T(8,128)}) fusion(f32[2,1,3,8,8,128]{3,5,4,2,1,0:T(8,128)S(1)} %pad_maximum_fusion, pred[]{:T(512)S(6)} %eq.49), kind=kLoop, calls=%fused_computation.3 | loop fusion | flops 49152 | bytes 589825 | tf_op jit(solution)/shard_map/stack;reshape | solution.py:24
  262.8 2.3 copy.79
  265.2 4.7 %collective-permute-start.13 = (f32[2,3,8,8,128]{4,3,2,1,0:T(8,128)S(1)}, f32[2,3,8,8,128]{4,3,2,1,0:T(8,128)S(1)}, u32[]{:S(2)}, u32[]{:S(2)}) collective-permute-start(f32[2,3,8,8,128]{4,3,2,1,0:T(8,128)S(1)} %copy.79), channel_id=1, source_target_pairs={{0,2},{1,3},{2,0},{3,1},{4,6},{5,7},{6,4},{7,5},{8,10},{9,11},{10,... | collective-permute-start | bytes 589832 | tf_op jit(solution)/shard_map/ppermute | solution.py:23
  269.8 1.3 collective-permute-start.15
  271.1 3.0 collective-permute-start.16
  274.2 2.3 copy.80
  276.6 2.4 collective-permute-start.14
  279.8 17.1 %collective-permute-done.14 = f32[4,3,8,8,128]{4,3,2,1,0:T(8,128)S(1)} collective-permute-done((f32[4,3,8,8,128]{4,3,2,1,0:T(8,128)S(1)}, f32[4,3,8,8,128]{4,3,2,1,0:T(8,128)S(1)}, u32[]{:S(2)}, u32[]{:S(2)}) %collective-permute-start.14) | collective-permute-done | bytes 393248 | tf_op jit(solution)/shard_map/ppermute | solution.py:23
  297.7 1.7 fusion.15
  299.9 1.3 collective-permute-start.17
  301.2 4.6 %collective-permute-start.18 = (f32[4,8,26,1]{3,2,1,0:T(8,128)S(1)}, f32[4,8,26,1]{3,2,1,0:T(8,128)S(1)}, u32[]{:S(2)}, u32[]{:S(2)}) collective-permute-start(f32[4,8,26,1]{3,2,1,0:T(8,128)S(1)} %get-tuple-element.49), channel_id=1, source_target_pairs={{0,1},{1,2},{2,3},{3,4},{4,5},{5,6},{6,7},{8,9},{9,10},{10,11},{11... | collective-permute-start | bytes 9992 | tf_op jit(solution)/shard_map/ppermute | solution.py:41
  305.8 9.9 %collective-permute-done.17 = f32[4,8,26,1]{3,2,1,0:T(8,128)S(1)} collective-permute-done((f32[4,8,26,1]{3,2,1,0:T(8,128)S(1)}, f32[4,8,26,1]{3,2,1,0:T(8,128)S(1)}, u32[]{:S(2)}, u32[]{:S(2)}) %collective-permute-start.17) | collective-permute-done | bytes 3360 | tf_op jit(solution)/shard_map/ppermute | solution.py:42
  315.7 10.3 %collective-permute-done.18 = f32[4,8,26,1]{3,2,1,0:T(8,128)S(1)} collective-permute-done((f32[4,8,26,1]{3,2,1,0:T(8,128)S(1)}, f32[4,8,26,1]{3,2,1,0:T(8,128)S(1)}, u32[]{:S(2)}, u32[]{:S(2)}) %collective-permute-start.18) | collective-permute-done | bytes 3360 | tf_op jit(solution)/shard_map/ppermute | solution.py:41
  326.0 1.2 fusion.21
  330.5 1.8 fusion.17
  (106 shorter events, 20.2 us)
Async XLA Ops:
  7.2 9.2 %copy-start = (f32[4,8,24,384]{3,2,1,0:T(8,128)S(1)}, f32[4,8,24,384]{3,2,1,0:T(8,128)}, u32[]{:S(2)}) copy-start(f32[4,8,24,384]{3,2,1,0:T(8,128)} %param.5) | copy-start | bytes 3538948
  7.2 64.1 %all-reduce.2.cloned.1.call-start = ((), (), s32[]{:S(2)}) async-start(), calls=%async_computation | async-start | bytes 196608 | tf_op jit(solution)/shard_map/psum | solution.py:107
  10.8 319.7 %all-gather.2.cloned.1.call-start = ((), (), s32[]{:S(2)}) async-start(), calls=%async_computation.1 | async-start | bytes 1474560 | tf_op jit(solution)/shard_map/all_gather | solution.py:147
  12.0 54.6 %collective-permute-start = (f32[4,8,1,384]{3,2,1,0:T(1,128)S(1)}, f32[4,8,1,384]{3,2,1,0:T(1,128)S(1)}, u32[]{:S(2)}, u32[]{:S(2)}) collective-permute-start(f32[4,8,1,384]{3,2,1,0:T(1,128)S(1)} %get-tuple-element.72), channel_id=1, source_target_pairs={{0,8},{8,16},{16,24},{1,9},{9,17},{17,25},{2,10},{10,18},{18,26},{... | collective-permute-start | bytes 147464 | tf_op jit(solution)/shard_map/ppermute | solution.py:41
  14.4 52.2 %collective-permute-start.1 = (f32[4,8,1,384]{3,2,1,0:T(1,128)S(1)}, f32[4,8,1,384]{3,2,1,0:T(1,128)S(1)}, u32[]{:S(2)}, u32[]{:S(2)}) collective-permute-start(f32[4,8,1,384]{3,2,1,0:T(1,128)S(1)} %get-tuple-element.73), channel_id=1, source_target_pairs={{8,0},{16,8},{24,16},{9,1},{17,9},{25,17},{10,2},{18,10},{26,18},{... | collective-permute-start | bytes 147464 | tf_op jit(solution)/shard_map/ppermute | solution.py:42
  16.7 49.9 %copy-start.1 = (f32[4,8,24,384]{3,2,1,0:T(8,128)S(1)}, f32[4,8,24,384]{3,2,1,0:T(8,128)}, u32[]{:S(2)}) copy-start(f32[4,8,24,384]{3,2,1,0:T(8,128)} %param.4) | copy-start | bytes 3538948
  67.9 56.3 %collective-permute-start.2 = (f32[4,8,26,1]{3,2,1,0:T(8,128)}, f32[4,8,26,1]{3,2,1,0:T(8,128)}, u32[]{:S(2)}, u32[]{:S(2)}) collective-permute-start(f32[4,8,26,1]{3,2,1,0:T(8,128)} %get-tuple-element.54), channel_id=1, source_target_pairs={{0,1},{1,2},{2,3},{3,4},{4,5},{5,6},{6,7},{8,9},{9,10},{10,11},{11... | collective-permute-start | bytes 9992 | tf_op jit(solution)/shard_map/ppermute | solution.py:41
  70.0 54.2 %collective-permute-start.3 = (f32[4,8,26,1]{3,2,1,0:T(8,128)}, f32[4,8,26,1]{3,2,1,0:T(8,128)}, u32[]{:S(2)}, u32[]{:S(2)}) collective-permute-start(f32[4,8,26,1]{3,2,1,0:T(8,128)} %get-tuple-element.55), channel_id=1, source_target_pairs={{1,0},{2,1},{3,2},{4,3},{5,4},{6,5},{7,6},{9,8},{10,9},{11,10},{12... | collective-permute-start | bytes 9992 | tf_op jit(solution)/shard_map/ppermute | solution.py:42
  129.6 2.6 collective-permute-start.4
  130.9 4.5 %collective-permute-start.5 = (f32[4,8,1,384]{3,2,1,0:T(1,128)S(1)}, f32[4,8,1,384]{3,2,1,0:T(1,128)S(1)}, u32[]{:S(2)}, u32[]{:S(2)}) collective-permute-start(f32[4,8,1,384]{3,2,1,0:T(1,128)S(1)} %get-tuple-element.69), channel_id=1, source_target_pairs={{8,0},{16,8},{24,16},{9,1},{17,9},{25,17},{10,2},{18,10},{26,18},{... | collective-permute-start | bytes 147464 | tf_op jit(solution)/shard_map/ppermute | solution.py:42
  135.8 22.7 %collective-permute-start.6 = (f32[4,8,26,1]{3,2,1,0:T(8,128)S(1)}, f32[4,8,26,1]{3,2,1,0:T(8,128)S(1)}, u32[]{:S(2)}, u32[]{:S(2)}) collective-permute-start(f32[4,8,26,1]{3,2,1,0:T(8,128)S(1)} %get-tuple-element.52), channel_id=1, source_target_pairs={{0,1},{1,2},{2,3},{3,4},{4,5},{5,6},{6,7},{8,9},{9,10},{10,11},{11... | collective-permute-start | bytes 9992 | tf_op jit(solution)/shard_map/ppermute | solution.py:41
  137.1 21.3 %collective-permute-start.7 = (f32[4,8,26,1]{3,2,1,0:T(8,128)S(1)}, f32[4,8,26,1]{3,2,1,0:T(8,128)S(1)}, u32[]{:S(2)}, u32[]{:S(2)}) collective-permute-start(f32[4,8,26,1]{3,2,1,0:T(8,128)S(1)} %get-tuple-element.53), channel_id=1, source_target_pairs={{1,0},{2,1},{3,2},{4,3},{5,4},{6,5},{7,6},{9,8},{10,9},{11,10},{12... | collective-permute-start | bytes 9992 | tf_op jit(solution)/shard_map/ppermute | solution.py:42
  163.5 5.5 %collective-permute-start.8 = (f32[4,8,1,384]{3,2,1,0:T(1,128)S(1)}, f32[4,8,1,384]{3,2,1,0:T(1,128)S(1)}, u32[]{:S(2)}, u32[]{:S(2)}) collective-permute-start(f32[4,8,1,384]{3,2,1,0:T(1,128)S(1)} %get-tuple-element.66), channel_id=1, source_target_pairs={{0,8},{8,16},{16,24},{1,9},{9,17},{17,25},{2,10},{10,18},{18,26},{... | collective-permute-start | bytes 147464 | tf_op jit(solution)/shard_map/ppermute | solution.py:41
  167.7 3.1 collective-permute-start.9
  171.1 26.1 %collective-permute-start.10 = (f32[4,8,26,1]{3,2,1,0:T(8,128)S(1)}, f32[4,8,26,1]{3,2,1,0:T(8,128)S(1)}, u32[]{:S(2)}, u32[]{:S(2)}) collective-permute-start(f32[4,8,26,1]{3,2,1,0:T(8,128)S(1)} %get-tuple-element.50), channel_id=1, source_target_pairs={{0,1},{1,2},{2,3},{3,4},{4,5},{5,6},{6,7},{8,9},{9,10},{10,11},{11... | collective-permute-start | bytes 9992 | tf_op jit(solution)/shard_map/ppermute | solution.py:41
  175.2 22.0 %collective-permute-start.11 = (f32[4,8,26,1]{3,2,1,0:T(8,128)S(1)}, f32[4,8,26,1]{3,2,1,0:T(8,128)S(1)}, u32[]{:S(2)}, u32[]{:S(2)}) collective-permute-start(f32[4,8,26,1]{3,2,1,0:T(8,128)S(1)} %get-tuple-element.51), channel_id=1, source_target_pairs={{1,0},{2,1},{3,2},{4,3},{5,4},{6,5},{7,6},{9,8},{10,9},{11,10},{12... | collective-permute-start | bytes 9992 | tf_op jit(solution)/shard_map/ppermute | solution.py:42
  202.7 8.3 %copy-start.2 = (f32[1,8,24,384]{3,2,1,0:T(8,128)}, f32[1,8,24,384]{3,2,1,0:T(8,128)S(1)}, u32[]{:S(2)}) copy-start(f32[1,8,24,384]{3,2,1,0:T(8,128)S(1)} %get-tuple-element.13) | copy-start | bytes 884740
  251.6 5.5 %collective-permute-start.12 = (f32[1,3,8,8,128]{4,3,2,1,0:T(8,128)S(1)}, f32[1,3,8,8,128]{4,3,2,1,0:T(8,128)S(1)}, u32[]{:S(2)}, u32[]{:S(2)}) collective-permute-start(f32[1,3,8,8,128]{4,3,2,1,0:T(8,128)S(1)} %copy.77), channel_id=1, source_target_pairs={{0,1},{1,0},{2,3},{3,2},{4,5},{5,4},{6,7},{7,6},{8,9},{9,8},{10,11... | collective-permute-start | bytes 294920 | tf_op jit(solution)/shard_map/ppermute | solution.py:23
  265.2 11.3 %collective-permute-start.13 = (f32[2,3,8,8,128]{4,3,2,1,0:T(8,128)S(1)}, f32[2,3,8,8,128]{4,3,2,1,0:T(8,128)S(1)}, u32[]{:S(2)}, u32[]{:S(2)}) collective-permute-start(f32[2,3,8,8,128]{4,3,2,1,0:T(8,128)S(1)} %copy.79), channel_id=1, source_target_pairs={{0,2},{1,3},{2,0},{3,1},{4,6},{5,7},{6,4},{7,5},{8,10},{9,11},{10,... | collective-permute-start | bytes 589832 | tf_op jit(solution)/shard_map/ppermute | solution.py:23
  269.8 29.8 %collective-permute-start.15 = (f32[4,8,1,384]{3,2,1,0:T(1,128)}, f32[4,8,1,384]{3,2,1,0:T(1,128)S(1)}, u32[]{:S(2)}, u32[]{:S(2)}) collective-permute-start(f32[4,8,1,384]{3,2,1,0:T(1,128)} %get-tuple-element.63), channel_id=1, source_target_pairs={{8,0},{16,8},{24,16},{9,1},{17,9},{25,17},{10,2},{18,10},{26,18},{... | collective-permute-start | bytes 147464 | tf_op jit(solution)/shard_map/ppermute | solution.py:42
  271.1 28.5 %collective-permute-start.16 = (f32[4,8,1,384]{3,2,1,0:T(1,128)}, f32[4,8,1,384]{3,2,1,0:T(1,128)S(1)}, u32[]{:S(2)}, u32[]{:S(2)}) collective-permute-start(f32[4,8,1,384]{3,2,1,0:T(1,128)} %get-tuple-element.62), channel_id=1, source_target_pairs={{0,8},{8,16},{16,24},{1,9},{9,17},{17,25},{2,10},{10,18},{18,26},{... | collective-permute-start | bytes 147464 | tf_op jit(solution)/shard_map/ppermute | solution.py:41
  276.6 20.4 %collective-permute-start.14 = (f32[4,3,8,8,128]{4,3,2,1,0:T(8,128)S(1)}, f32[4,3,8,8,128]{4,3,2,1,0:T(8,128)S(1)}, u32[]{:S(2)}, u32[]{:S(2)}) collective-permute-start(f32[4,3,8,8,128]{4,3,2,1,0:T(8,128)S(1)} %bitcast.105), channel_id=1, source_target_pairs={{0,4},{1,5},{2,6},{3,7},{4,0},{5,1},{6,2},{7,3},{8,12},{9,13},{10,... | collective-permute-start | bytes 1179656 | tf_op jit(solution)/shard_map/ppermute | solution.py:23
  299.9 15.8 %collective-permute-start.17 = (f32[4,8,26,1]{3,2,1,0:T(8,128)S(1)}, f32[4,8,26,1]{3,2,1,0:T(8,128)S(1)}, u32[]{:S(2)}, u32[]{:S(2)}) collective-permute-start(f32[4,8,26,1]{3,2,1,0:T(8,128)S(1)} %get-tuple-element.48), channel_id=1, source_target_pairs={{1,0},{2,1},{3,2},{4,3},{5,4},{6,5},{7,6},{9,8},{10,9},{11,10},{12... | collective-permute-start | bytes 9992 | tf_op jit(solution)/shard_map/ppermute | solution.py:42
  301.2 24.8 %collective-permute-start.18 = (f32[4,8,26,1]{3,2,1,0:T(8,128)S(1)}, f32[4,8,26,1]{3,2,1,0:T(8,128)S(1)}, u32[]{:S(2)}, u32[]{:S(2)}) collective-permute-start(f32[4,8,26,1]{3,2,1,0:T(8,128)S(1)} %get-tuple-element.49), channel_id=1, source_target_pairs={{0,1},{1,2},{2,3},{3,4},{4,5},{5,6},{6,7},{8,9},{9,10},{10,11},{11... | collective-permute-start | bytes 9992 | tf_op jit(solution)/shard_map/ppermute | solution.py:41
  327.2 0.9 copy-start.5
  327.2 1.1 copy-start.6
  328.3 1.0 copy-start.3
  328.3 1.0 copy-start.4
Sparse Core Ops, SparseCore 0:
  10.9 34.0 all-reduce.1
  299.6 15.6 all-gather.1
